TPU v7x, 32 devices: a whole 2x2x4 slice. The times are simulated.
32 devices in a mesh: groups: 2 (over x), gx: 8 (over z, y), gy: 2 (over core).
Axes of the slice: x: 2, y: 2, z: 4, core: 2. Of those that a mesh axis runs over, the one named last changes fastest.
Arguments:
- features: bfloat16 [65536, 512], P(('groups', 'gx', 'gy')), parts along dimension 0, may hold values from -8 to 8
- norm_gain: float32 [512], replicated, may hold values from 0.25 to 1.75
- query_weight: bfloat16 [512, 512], replicated, may hold values from -40 to 40
- key_weight: bfloat16 [512, 512], replicated, may hold values from -1 to 1
- value_weight: bfloat16 [512, 512], replicated, may hold values from -0.25 to 0.25
- output_weight: bfloat16 [512, 512], replicated, may hold values from -0.25 to 0.25
- virtual_query: bfloat16 [16, 512], replicated, may hold values from -6 to 6
- tile_list: int32 [512, 6], P(('groups', 'gx', 'gy')), parts along dimension 0, may hold values from 0 to 63, as said below
- tile_count: int32 [512], P(('groups', 'gx', 'gy')), parts along dimension 0, may hold values from 1 to 6, as said below
- member_list: int32 [512, 4], P(('groups', 'gx', 'gy')), parts along dimension 0, may hold values from 0 to 15, as said below
- member_count: int32 [512], P(('groups', 'gx', 'gy')), parts along dimension 0, may hold values from 1 to 4
Outputs:
- attended: bfloat16 [65536, 512], P(('groups', 'gx', 'gy')), parts along dimension 0
There are 2 independent parts, one for each index of `groups`. A program takes and returns all parts, laid end to end along the dimension named above; an argument that names none is the same for every part. Nothing has to cross between parts.
Inputs may be any that keep to these rules, and one draw needn't show every extreme that they name: `tile_list`: the entries of a row are distinct, and the first is the block's own index b % 16. `tile_count`: in every draw the blocks of some partitions all have 6. `member_list`: the first member_count[b] entries of row b are distinct and lie in (a - 2 + k) mod 16 for k = 0..7, where a = b * 16 // 256; the remaining entries are valid ids that are not used.
All inputs are finite; a program needn't handle non-finite values.
Results may differ from a plain program's by a relative error of at most 0.0047.
Values may be sent and summed in bfloat16 or wider, within the bound.
A program may use at most 192 MiB of HBM per device.

v0:
```python
import math

import jax
import jax.numpy as jnp
from jax import lax
from jax.sharding import PartitionSpec as P

HEADS = 8
BLOCK = 128


def passed_along(block, axis, distance):
    devices = range(lax.axis_size(axis))
    route = [(i - distance, i) for i in devices if i - distance in devices]
    return lax.ppermute(block, axis, route)


def from_partner(value, axis, distance):
    mask = 2**distance
    pairs = [(source, source ^ mask) for source in range(lax.axis_size(axis))]
    return lax.ppermute(value, axis, pairs)


def combined_all(array, axis, join):
    gathered = jax.tree.map(
        lambda a, kind: lax.all_gather(a.astype(kind), axis),
        array,
        (jnp.bfloat16, jnp.bfloat16, jnp.bfloat16),
    )

    def take(source):
        return jax.tree.map(
            lambda a, own: lax.dynamic_index_in_dim(a, source, 0, False).astype(own.dtype),
            gathered,
            array,
        )

    return lax.fori_loop(
        1, lax.axis_size(axis), lambda source, state: join(state, take(source)), take(0)
    )


def normalize_rows(values, norm_gain):
    widened = values.astype(jnp.float32)
    scaled = widened * lax.rsqrt(jnp.mean(widened * widened, axis=-1, keepdims=True) + 1e-05)
    return (scaled * norm_gain).astype(jnp.bfloat16)


def project(source, weight):
    return jnp.dot(source, weight, preferred_element_type=jnp.float32).astype(jnp.bfloat16)


def expand_scale(scale_table, numerator):
    head_count = scale_table.shape[-1]
    split_view = numerator.reshape(numerator.shape[:-1] + (head_count, -1))
    return (split_view * scale_table[..., None]).reshape(numerator.shape)


def combine_parts(first_part, second_part):
    first_max, first_total, first_numer = first_part
    second_max, second_total, second_numer = second_part
    highest = jnp.maximum(first_max, second_max)
    first_scale = jnp.exp(first_max - highest)
    second_scale = jnp.exp(second_max - highest)
    total_sum = first_total * first_scale + second_total * second_scale
    numer_sum = expand_scale(first_scale, first_numer) + expand_scale(second_scale, second_numer)
    return (highest, total_sum, numer_sum)


def finish_virtual(parts, self_scores, self_values):
    unit_total = jnp.ones_like(self_scores)
    highest, total_sum, numer_sum = combine_parts(
        parts, (self_scores, unit_total, self_values.astype(jnp.float32))
    )
    return expand_scale(1.0 / total_sum, numer_sum).astype(jnp.bfloat16)


def virtual_partials(virt_queries, keys_own, values_own, member_list, member_count):
    virt_total = virt_queries.shape[0]
    slot_total = member_list.shape[1]
    head_size = keys_own.shape[1] // HEADS
    scaling = head_size ** (-0.5)
    targets = jnp.arange(virt_total, dtype=jnp.int32)
    listed = (member_list[None, :, :] == targets[:, None, None]) & (
        jnp.arange(slot_total, dtype=jnp.int32)[None, None, :] < member_count[None, :, None]
    )
    inside = jnp.repeat(jnp.any(listed, axis=2), BLOCK, axis=1)
    maxima = []
    totals = []
    numerators = []
    for head_index in range(HEADS):
        column = slice(head_index * head_size, (head_index + 1) * head_size)
        scores = (
            jnp.einsum(
                "ud,rd->ur",
                virt_queries[:, column],
                keys_own[:, column],
                preferred_element_type=jnp.float32,
            )
            * scaling
        )
        local_max = jnp.max(jnp.where(inside, scores, -1e30), axis=1)
        weights = jnp.where(inside, jnp.exp(scores - local_max[:, None]), 0.0)
        maxima.append(local_max)
        totals.append(jnp.sum(weights, axis=1))
        numerators.append(
            jnp.dot(
                weights, values_own[:, column].astype(jnp.float32), precision=lax.Precision.HIGHEST
            )
        )
    return (
        jnp.stack(maxima, axis=1),
        jnp.stack(totals, axis=1),
        jnp.concatenate(numerators, axis=1),
    )


def group_attention(
    query_group, tile_rows, count_group, pool_key_blocks, pool_value_blocks, virt_keys, virt_values
):
    group_size, _, width = query_group.shape
    head_size = width // HEADS
    slot_total = tile_rows.shape[1]
    scaling = head_size ** (-0.5)
    query_heads = query_group.reshape(group_size, BLOCK, HEADS, head_size)
    tile_keys = pool_key_blocks[tile_rows].reshape(group_size, slot_total * BLOCK, HEADS, head_size)
    tile_values = pool_value_blocks[tile_rows].reshape(
        group_size, slot_total * BLOCK, HEADS, head_size
    )
    virt_key_heads = virt_keys.reshape(-1, HEADS, head_size)
    virt_value_heads = virt_values.reshape(-1, HEADS, head_size)
    tile_scores = (
        jnp.einsum("gqhd,gkhd->ghqk", query_heads, tile_keys, preferred_element_type=jnp.float32)
        * scaling
    )
    virt_scores = (
        jnp.einsum(
            "gqhd,khd->ghqk", query_heads, virt_key_heads, preferred_element_type=jnp.float32
        )
        * scaling
    )
    slot_of_key = jnp.arange(slot_total * BLOCK, dtype=jnp.int32) // BLOCK
    live = (slot_of_key[None, :] < count_group[:, None])[:, None, None, :]
    highest = jnp.maximum(
        jnp.max(jnp.where(live, tile_scores, -1e30), axis=3), jnp.max(virt_scores, axis=3)
    )
    tile_weights = jnp.where(live, jnp.exp(tile_scores - highest[..., None]), 0.0)
    virt_weights = jnp.exp(virt_scores - highest[..., None])
    total_sum = jnp.sum(tile_weights, axis=3) + jnp.sum(virt_weights, axis=3)
    numerator = jnp.einsum(
        "ghqk,gkhd->gqhd",
        tile_weights.astype(jnp.bfloat16),
        tile_values,
        preferred_element_type=jnp.float32,
    )
    numerator = numerator + jnp.einsum(
        "ghqk,khd->gqhd",
        virt_weights.astype(jnp.bfloat16),
        virt_value_heads,
        preferred_element_type=jnp.float32,
    )
    scaled = numerator / jnp.transpose(total_sum, (0, 2, 1))[..., None]
    return scaled.reshape(group_size, BLOCK, width).astype(jnp.bfloat16)


def body(
    features,
    norm_gain,
    query_weight,
    key_weight,
    value_weight,
    output_weight,
    virtual_query,
    tile_list,
    tile_count,
    member_list,
    member_count,
):
    width = features.shape[1]
    head_size = width // HEADS
    scaling = head_size ** (-0.5)
    normed = normalize_rows(features, norm_gain)
    queries = project(normed, query_weight)
    keys_own = project(normed, key_weight)
    values_own = project(normed, value_weight)
    lower_keys, lower_values = passed_along((keys_own, values_own), "gx", 1)
    upper_keys, upper_values = passed_along((keys_own, values_own), "gx", -1)
    partner_keys, partner_values = from_partner((keys_own, values_own), "gy", 0)
    pool_keys = jnp.concatenate([keys_own, lower_keys, upper_keys, partner_keys], axis=0)
    pool_values = jnp.concatenate([values_own, lower_values, upper_values, partner_values], axis=0)
    virt_normed = normalize_rows(virtual_query, norm_gain)
    virt_queries = project(virt_normed, query_weight)
    virt_self_keys = project(virt_normed, key_weight)
    virt_self_values = project(virt_normed, value_weight)
    virt_total = virt_queries.shape[0]
    self_scores = (
        jnp.sum(
            (virt_queries.astype(jnp.float32) * virt_self_keys.astype(jnp.float32)).reshape(
                virt_total, HEADS, head_size
            ),
            axis=2,
        )
        * scaling
    )
    part_max, part_total, part_numer = virtual_partials(
        virt_queries, keys_own, values_own, member_list, member_count
    )
    merged = combined_all((part_max, part_total, part_numer), ("gx", "gy"), combine_parts)
    aggregate = finish_virtual(merged, self_scores, virt_self_values)
    virt_keys = project(aggregate, key_weight)
    virt_values = project(aggregate, value_weight)
    blocks_here = tile_list.shape[0]
    group_size = math.gcd(4, blocks_here)
    group_total = blocks_here // group_size
    pool_key_blocks = pool_keys.reshape(-1, BLOCK, width)
    pool_value_blocks = pool_values.reshape(-1, BLOCK, width)

    def attend(packed):
        query_group, tile_rows, count_group = packed
        return group_attention(
            query_group,
            tile_rows,
            count_group,
            pool_key_blocks,
            pool_value_blocks,
            virt_keys,
            virt_values,
        )

    grouped = (
        queries.reshape(group_total, group_size, BLOCK, width),
        tile_list.reshape(group_total, group_size, -1),
        tile_count.reshape(group_total, group_size),
    )
    mixed = lax.map(attend, grouped).reshape(blocks_here * BLOCK, width)
    return (
        features.astype(jnp.float32)
        + jnp.dot(mixed, output_weight, preferred_element_type=jnp.float32)
    ).astype(jnp.bfloat16)


def solution(mesh):
    placed = (
        P(("groups", "gx", "gy"), None),
        P(),
        P(),
        P(),
        P(),
        P(),
        P(),
        P(("groups", "gx", "gy"), None),
        P(("groups", "gx", "gy")),
        P(("groups", "gx", "gy"), None),
        P(("groups", "gx", "gy")),
    )
    return jax.shard_map(
        body, mesh=mesh, in_specs=placed, out_specs=P(("groups", "gx", "gy"), None), check_vma=False
    )
```

profile of v0, /device:TPU:13, one launch (start us, length us, event | category | flops | bytes accessed | tf_op | source)
XLA Modules:
  0.0 554.0 jit_solution(5024753136054418619)
XLA Ops:
  0.0 2.1 fusion.37
  2.2 3.3 convolution_convert_fusion
  5.5 3.3 collective-permute-start.3
  8.8 2.1 collective-permute-start.4
  10.9 1.3 collective-permute-start.5
  12.2 2.8 convolution_convert_fusion.2
  15.1 4.2 collective-permute-start
  19.2 1.9 collective-permute-start.1
  23.4 1.3 fusion.48
  24.7 1.3 fusion.49
  26.1 1.3 fusion.50
  27.4 1.3 fusion.51
  28.8 1.3 fusion.52
  30.1 1.4 fusion.53
  31.5 1.3 fusion.54
  32.9 1.4 fusion.55
  34.8 166.6 %all_gather.14 = bf16[16,16,512]{2,1,0:T(8,128)(2,1)S(1)} all-gather(bf16[1,16,512]{2,1,0:T(8,128)(2,1)S(1)} %concatenate.59), channel_id=1, replica_groups=mesh['groups'=2,'gx'=8,'gy'=2] {'gx','gy'}, dimensions={0}, use_global_device_ids=true | all-gather | bytes 278528 | tf_op jit(solution)/shard_map/all_gather | solution.py:26
  202.1 16.9 %all_gather.13 = bf16[16,16,8]{1,2,0:T(8,128)(2,1)S(1)} all-gather(bf16[1,16,8]{1,2,0:T(8,128)(2,1)S(1)} %stack.71), channel_id=1, replica_groups=mesh['groups'=2,'gx'=8,'gy'=2] {'gx','gy'}, dimensions={0}, use_global_device_ids=true | all-gather | bytes 4352 | tf_op jit(solution)/shard_map/all_gather | solution.py:26
  219.1 19.5 %all_gather.12 = bf16[16,16,8]{1,2,0:T(8,128)(2,1)S(1)} all-gather(bf16[1,16,8]{1,2,0:T(8,128)(2,1)S(1)} %stack.62), channel_id=1, replica_groups=mesh['groups'=2,'gx'=8,'gy'=2] {'gx','gy'}, dimensions={0}, use_global_device_ids=true | all-gather | bytes 4352 | tf_op jit(solution)/shard_map/all_gather | solution.py:26
  238.7 18.7 %while.31 = (s32[]{:T(128)}, f32[16,8]{0,1:T(8,128)S(1)}, f32[16,8]{0,1:T(8,128)S(1)}, f32[16,512]{1,0:T(8,128)S(1)}, bf16[16,16,8]{1,2,0:T(8,128)(2,1)S(1)}, /*...) while((s32[]{:T(128)}, f32[16,8]{0,1:T(8,128)S(1)}, ...), condition=%wide.region_20.21_spmd, body=%wide.region_19.20_spmd.sunk | while | flops 33797 | bytes 350871 | solution.py:38
  259.5 4.3 convolution_convert_fusion.1
  263.8 6.5 %pad_maximum_fusion.1 = bf16[8192,512]{0,1:T(8,128)(2,1)} fusion(bf16[2048,512]{0,1:T(8,128)(2,1)} %collective-permute-done.5, bf16[2048,512]{0,1:T(8,128)(2,1)} %collective-permute-done.4, bf16[2048,512]{0,1:T(8,128)(2,1)} %collective-permute-done.3, bf16[2048,512]{0,1:T(8,128)(2,1)S(1)} %convolution_convert_fusion), kind=kLoop, calls=%fused_computation.57 | loop fusion | flops 33554432 | bytes 16777216 | tf_op jit(solution)/shard_map/concatenate | solution.py:189
  270.3 12.0 %copy.143 = bf16[8192,512]{1,0:T(8,128)(2,1)} copy(bf16[8192,512]{0,1:T(8,128)(2,1)} %pad_maximum_fusion.1) | data formatting | bytes 16777216 | tf_op jit(solution)/shard_map/while | solution.py:235
  282.3 7.0 %pad_maximum_fusion = bf16[8192,512]{0,1:T(8,128)(2,1)} fusion(bf16[2048,512]{0,1:T(8,128)(2,1)} %collective-permute-done.2, bf16[2048,512]{0,1:T(8,128)(2,1)} %collective-permute-done.1, bf16[2048,512]{0,1:T(8,128)(2,1)} %collective-permute-done, bf16[2048,512]{0,1:T(8,128)(2,1)} %convolution_convert_fusion.2), kind=kLoop, calls=%fused_computation.56 | loop fusion | flops 33554432 | bytes 16777216 | tf_op jit(solution)/shard_map/concatenate | solution.py:190
  289.3 11.9 %copy.142 = bf16[8192,512]{1,0:T(8,128)(2,1)} copy(bf16[8192,512]{0,1:T(8,128)(2,1)} %pad_maximum_fusion) | data formatting | bytes 16777216 | tf_op jit(solution)/shard_map/while | solution.py:235
  301.2 248.4 %while.32 = (s32[]{:T(128)}, bf16[4,4,128,512]{3,2,1,0:T(8,128)(2,1)}, s32[4,4,6]{2,1,0:T(4,128)S(1)}, bf16[64,128,512]{2,1,0:T(8,128)(2,1)}, s32[4,4]{1,0:T(4,1...) while((s32[]{:T(128)}, ...), condition=%wide.region_27.28_spmd, body=%wide.region_22.27_spmd.sunk | while | flops 857802816 | bytes 78241088 | solution.py:235
  301.3 6.0 %gather_fusion = bf16[24,128,512]{2,1,0:T(8,128)(2,1)} fusion(bf16[64,128,512]{2,1,0:T(8,128)(2,1)} %get-tuple-element.599, s32[1024]{0:T(1024)S(1)} %pad_clamp_fusion.2), kind=kCustom, calls=%fused_computation.1.clone.1 | custom fusion | bytes 6291552 | tf_op jit(solution)/shard_map/while/body/eval_jaxpr/gather | solution.py:126
  307.3 8.9 %reshape.675 = bf16[4,768,8,64]{3,2,1,0:T(8,128)(2,1)} reshape(bf16[24,128,512]{2,1,0:T(8,128)(2,1)} %gather_fusion) | data formatting | bytes 6291456 | tf_op jit(solution)/shard_map/while/body/eval_jaxpr/reshape | solution.py:126
  316.3 1.1 constant_dynamic-slice_fusion.3
  317.7 10.4 %select_reduce_fusion.10 = (f32[4,8,128]{2,1,0:T(8,128)S(1)}, f32[4,8,128,768]{3,2,1,0:T(8,128)}) fusion(pred[4,768]{1,0:T(4,128)(4,1)S(1)} %broadcast_compare_fusion.2, bf16[4,128,8,64]{1,3,2,0:T(8,128)(2,1)S(1)} %bitcast.193, bf16[4,768,8,64]{3,2,1,0:T(8,128)(2,1)} %reshape.675), kind=kOutput, calls=%fused_computation.11.clone.1 | convolution fusion | flops 412086272 | bytes 16272384 | tf_op jit(solution)/shard_map/while/body/eval_jaxpr/gqhd,gkhd->ghqk/dot_general | solution.py:133
  328.4 6.5 %fusion.177 = f32[4,8,128]{2,1,0:T(8,128)S(1)} fusion(f32[4,8,128,768]{3,2,1,0:T(8,128)} %get-tuple-element.537, f32[4,8,128]{2,1,0:T(8,128)S(1)} %copy_maximum_fusion.2, pred[4,768]{1,0:T(4,128)(4,1)S(1)} %broadcast_compare_fusion.2), kind=kLoop, calls=%fused_computation.12.clone.1 | loop fusion | flops 12578816 | bytes 12618752 | tf_op jit(solution)/shard_map/while/body/eval_jaxpr/reduce_sum | solution.py:149
  335.1 5.9 %gather_fusion.1 = bf16[24,128,512]{2,1,0:T(8,128)(2,1)} fusion(bf16[64,128,512]{2,1,0:T(8,128)(2,1)} %get-tuple-element.596, s32[1024]{0:T(1024)S(1)} %pad_clamp_fusion.2), kind=kCustom, calls=%fused_computation.clone.1 | custom fusion | bytes 6291552 | tf_op jit(solution)/shard_map/while/body/eval_jaxpr/gather | solution.py:127
  341.0 8.9 %reshape.677 = bf16[4,768,8,64]{3,2,1,0:T(8,128)(2,1)} reshape(bf16[24,128,512]{2,1,0:T(8,128)(2,1)} %gather_fusion.1) | data formatting | bytes 6291456 | tf_op jit(solution)/shard_map/while/body/eval_jaxpr/reshape | solution.py:127
  349.9 10.8 %fusion.176 = f32[4,128,8,64]{1,3,2,0:T(8,128)} fusion(f32[4,8,128,768]{3,2,1,0:T(8,128)} %get-tuple-element.537, f32[4,8,128]{2,1,0:T(8,128)S(1)} %copy_maximum_fusion.2, pred[4,768]{1,0:T(4,128)(4,1)S(1)} %broadcast_compare_fusion.2, bf16[4,768,8,64]{3,2,1,0:T(8,128)(2,1)} %reshape.677), kind=kOutput, calls=%fused_computation.22.clone.1 | convolution fusion | flops 415236096 | bytes 16796672 | tf_op jit(solution)/shard_map/while/body/eval_jaxpr/ghqk,gkhd->gqhd/dot_general | solution.py:150
  360.8 1.6 fusion.180
  363.5 5.9 %gather_fusion = bf16[24,128,512]{2,1,0:T(8,128)(2,1)} fusion(bf16[64,128,512]{2,1,0:T(8,128)(2,1)} %get-tuple-element.599, s32[1024]{0:T(1024)S(1)} %pad_clamp_fusion.2), kind=kCustom, calls=%fused_computation.1.clone.1 | custom fusion | bytes 6291552 | tf_op jit(solution)/shard_map/while/body/eval_jaxpr/gather | solution.py:126
  369.4 8.9 %reshape.675 = bf16[4,768,8,64]{3,2,1,0:T(8,128)(2,1)} reshape(bf16[24,128,512]{2,1,0:T(8,128)(2,1)} %gather_fusion) | data formatting | bytes 6291456 | tf_op jit(solution)/shard_map/while/body/eval_jaxpr/reshape | solution.py:126
  378.4 1.1 constant_dynamic-slice_fusion.3
  379.7 10.4 %select_reduce_fusion.10 = (f32[4,8,128]{2,1,0:T(8,128)S(1)}, f32[4,8,128,768]{3,2,1,0:T(8,128)}) fusion(pred[4,768]{1,0:T(4,128)(4,1)S(1)} %broadcast_compare_fusion.2, bf16[4,128,8,64]{1,3,2,0:T(8,128)(2,1)S(1)} %bitcast.193, bf16[4,768,8,64]{3,2,1,0:T(8,128)(2,1)} %reshape.675), kind=kOutput, calls=%fused_computation.11.clone.1 | convolution fusion | flops 412086272 | bytes 16272384 | tf_op jit(solution)/shard_map/while/body/eval_jaxpr/gqhd,gkhd->ghqk/dot_general | solution.py:133
  390.5 6.5 %fusion.177 = f32[4,8,128]{2,1,0:T(8,128)S(1)} fusion(f32[4,8,128,768]{3,2,1,0:T(8,128)} %get-tuple-element.537, f32[4,8,128]{2,1,0:T(8,128)S(1)} %copy_maximum_fusion.2, pred[4,768]{1,0:T(4,128)(4,1)S(1)} %broadcast_compare_fusion.2), kind=kLoop, calls=%fused_computation.12.clone.1 | loop fusion | flops 12578816 | bytes 12618752 | tf_op jit(solution)/shard_map/while/body/eval_jaxpr/reduce_sum | solution.py:149
  397.2 5.9 %gather_fusion.1 = bf16[24,128,512]{2,1,0:T(8,128)(2,1)} fusion(bf16[64,128,512]{2,1,0:T(8,128)(2,1)} %get-tuple-element.596, s32[1024]{0:T(1024)S(1)} %pad_clamp_fusion.2), kind=kCustom, calls=%fused_computation.clone.1 | custom fusion | bytes 6291552 | tf_op jit(solution)/shard_map/while/body/eval_jaxpr/gather | solution.py:127
  403.1 8.9 %reshape.677 = bf16[4,768,8,64]{3,2,1,0:T(8,128)(2,1)} reshape(bf16[24,128,512]{2,1,0:T(8,128)(2,1)} %gather_fusion.1) | data formatting | bytes 6291456 | tf_op jit(solution)/shard_map/while/body/eval_jaxpr/reshape | solution.py:127
  412.0 10.8 %fusion.176 = f32[4,128,8,64]{1,3,2,0:T(8,128)} fusion(f32[4,8,128,768]{3,2,1,0:T(8,128)} %get-tuple-element.537, f32[4,8,128]{2,1,0:T(8,128)S(1)} %copy_maximum_fusion.2, pred[4,768]{1,0:T(4,128)(4,1)S(1)} %broadcast_compare_fusion.2, bf16[4,768,8,64]{3,2,1,0:T(8,128)(2,1)} %reshape.677), kind=kOutput, calls=%fused_computation.22.clone.1 | convolution fusion | flops 415236096 | bytes 16796672 | tf_op jit(solution)/shard_map/while/body/eval_jaxpr/ghqk,gkhd->gqhd/dot_general | solution.py:150
  422.9 1.6 fusion.180
  425.6 5.9 %gather_fusion = bf16[24,128,512]{2,1,0:T(8,128)(2,1)} fusion(bf16[64,128,512]{2,1,0:T(8,128)(2,1)} %get-tuple-element.599, s32[1024]{0:T(1024)S(1)} %pad_clamp_fusion.2), kind=kCustom, calls=%fused_computation.1.clone.1 | custom fusion | bytes 6291552 | tf_op jit(solution)/shard_map/while/body/eval_jaxpr/gather | solution.py:126
  431.5 8.9 %reshape.675 = bf16[4,768,8,64]{3,2,1,0:T(8,128)(2,1)} reshape(bf16[24,128,512]{2,1,0:T(8,128)(2,1)} %gather_fusion) | data formatting | bytes 6291456 | tf_op jit(solution)/shard_map/while/body/eval_jaxpr/reshape | solution.py:126
  440.5 1.1 constant_dynamic-slice_fusion.3
  441.8 10.4 %select_reduce_fusion.10 = (f32[4,8,128]{2,1,0:T(8,128)S(1)}, f32[4,8,128,768]{3,2,1,0:T(8,128)}) fusion(pred[4,768]{1,0:T(4,128)(4,1)S(1)} %broadcast_compare_fusion.2, bf16[4,128,8,64]{1,3,2,0:T(8,128)(2,1)S(1)} %bitcast.193, bf16[4,768,8,64]{3,2,1,0:T(8,128)(2,1)} %reshape.675), kind=kOutput, calls=%fused_computation.11.clone.1 | convolution fusion | flops 412086272 | bytes 16272384 | tf_op jit(solution)/shard_map/while/body/eval_jaxpr/gqhd,gkhd->ghqk/dot_general | solution.py:133
  452.6 6.5 %fusion.177 = f32[4,8,128]{2,1,0:T(8,128)S(1)} fusion(f32[4,8,128,768]{3,2,1,0:T(8,128)} %get-tuple-element.537, f32[4,8,128]{2,1,0:T(8,128)S(1)} %copy_maximum_fusion.2, pred[4,768]{1,0:T(4,128)(4,1)S(1)} %broadcast_compare_fusion.2), kind=kLoop, calls=%fused_computation.12.clone.1 | loop fusion | flops 12578816 | bytes 12618752 | tf_op jit(solution)/shard_map/while/body/eval_jaxpr/reduce_sum | solution.py:149
  459.2 5.9 %gather_fusion.1 = bf16[24,128,512]{2,1,0:T(8,128)(2,1)} fusion(bf16[64,128,512]{2,1,0:T(8,128)(2,1)} %get-tuple-element.596, s32[1024]{0:T(1024)S(1)} %pad_clamp_fusion.2), kind=kCustom, calls=%fused_computation.clone.1 | custom fusion | bytes 6291552 | tf_op jit(solution)/shard_map/while/body/eval_jaxpr/gather | solution.py:127
  465.2 8.9 %reshape.677 = bf16[4,768,8,64]{3,2,1,0:T(8,128)(2,1)} reshape(bf16[24,128,512]{2,1,0:T(8,128)(2,1)} %gather_fusion.1) | data formatting | bytes 6291456 | tf_op jit(solution)/shard_map/while/body/eval_jaxpr/reshape | solution.py:127
  474.1 10.8 %fusion.176 = f32[4,128,8,64]{1,3,2,0:T(8,128)} fusion(f32[4,8,128,768]{3,2,1,0:T(8,128)} %get-tuple-element.537, f32[4,8,128]{2,1,0:T(8,128)S(1)} %copy_maximum_fusion.2, pred[4,768]{1,0:T(4,128)(4,1)S(1)} %broadcast_compare_fusion.2, bf16[4,768,8,64]{3,2,1,0:T(8,128)(2,1)} %reshape.677), kind=kOutput, calls=%fused_computation.22.clone.1 | convolution fusion | flops 415236096 | bytes 16796672 | tf_op jit(solution)/shard_map/while/body/eval_jaxpr/ghqk,gkhd->gqhd/dot_general | solution.py:150
  484.9 1.6 fusion.180
  486.7 0.9 constant_dynamic-update-slice_fusion.2
  487.7 5.9 %gather_fusion = bf16[24,128,512]{2,1,0:T(8,128)(2,1)} fusion(bf16[64,128,512]{2,1,0:T(8,128)(2,1)} %get-tuple-element.599, s32[1024]{0:T(1024)S(1)} %pad_clamp_fusion.2), kind=kCustom, calls=%fused_computation.1.clone.1 | custom fusion | bytes 6291552 | tf_op jit(solution)/shard_map/while/body/eval_jaxpr/gather | solution.py:126
  493.6 8.9 %reshape.675 = bf16[4,768,8,64]{3,2,1,0:T(8,128)(2,1)} reshape(bf16[24,128,512]{2,1,0:T(8,128)(2,1)} %gather_fusion) | data formatting | bytes 6291456 | tf_op jit(solution)/shard_map/while/body/eval_jaxpr/reshape | solution.py:126
  502.6 1.1 constant_dynamic-slice_fusion.3
  503.9 10.4 %select_reduce_fusion.10 = (f32[4,8,128]{2,1,0:T(8,128)S(1)}, f32[4,8,128,768]{3,2,1,0:T(8,128)}) fusion(pred[4,768]{1,0:T(4,128)(4,1)S(1)} %broadcast_compare_fusion.2, bf16[4,128,8,64]{1,3,2,0:T(8,128)(2,1)S(1)} %bitcast.193, bf16[4,768,8,64]{3,2,1,0:T(8,128)(2,1)} %reshape.675), kind=kOutput, calls=%fused_computation.11.clone.1 | convolution fusion | flops 412086272 | bytes 16272384 | tf_op jit(solution)/shard_map/while/body/eval_jaxpr/gqhd,gkhd->ghqk/dot_general | solution.py:133
  514.7 6.5 %fusion.177 = f32[4,8,128]{2,1,0:T(8,128)S(1)} fusion(f32[4,8,128,768]{3,2,1,0:T(8,128)} %get-tuple-element.537, f32[4,8,128]{2,1,0:T(8,128)S(1)} %copy_maximum_fusion.2, pred[4,768]{1,0:T(4,128)(4,1)S(1)} %broadcast_compare_fusion.2), kind=kLoop, calls=%fused_computation.12.clone.1 | loop fusion | flops 12578816 | bytes 12618752 | tf_op jit(solution)/shard_map/while/body/eval_jaxpr/reduce_sum | solution.py:149
  521.3 5.9 %gather_fusion.1 = bf16[24,128,512]{2,1,0:T(8,128)(2,1)} fusion(bf16[64,128,512]{2,1,0:T(8,128)(2,1)} %get-tuple-element.596, s32[1024]{0:T(1024)S(1)} %pad_clamp_fusion.2), kind=kCustom, calls=%fused_computation.clone.1 | custom fusion | bytes 6291552 | tf_op jit(solution)/shard_map/while/body/eval_jaxpr/gather | solution.py:127
  527.3 8.9 %reshape.677 = bf16[4,768,8,64]{3,2,1,0:T(8,128)(2,1)} reshape(bf16[24,128,512]{2,1,0:T(8,128)(2,1)} %gather_fusion.1) | data formatting | bytes 6291456 | tf_op jit(solution)/shard_map/while/body/eval_jaxpr/reshape | solution.py:127
  536.2 10.8 %fusion.176 = f32[4,128,8,64]{1,3,2,0:T(8,128)} fusion(f32[4,8,128,768]{3,2,1,0:T(8,128)} %get-tuple-element.537, f32[4,8,128]{2,1,0:T(8,128)S(1)} %copy_maximum_fusion.2, pred[4,768]{1,0:T(4,128)(4,1)S(1)} %broadcast_compare_fusion.2, bf16[4,768,8,64]{3,2,1,0:T(8,128)(2,1)} %reshape.677), kind=kOutput, calls=%fused_computation.22.clone.1 | convolution fusion | flops 415236096 | bytes 16796672 | tf_op jit(solution)/shard_map/while/body/eval_jaxpr/ghqk,gkhd->gqhd/dot_general | solution.py:150
  547.0 1.6 fusion.180
  549.7 4.4 fusion.40
  (262 shorter events, 31.1 us)
Async XLA Ops:
  0.0 12.2 %copy-start = (bf16[512,512]{1,0:T(8,128)(2,1)S(1)}, bf16[512,512]{1,0:T(8,128)(2,1)}, u32[]{:S(2)}) copy-start(bf16[512,512]{1,0:T(8,128)(2,1)} %param.19) | copy-start | bytes 1572868
  2.1 10.1 %copy-start.2 = (bf16[2048,512]{1,0:T(8,128)(2,1)S(1)}, bf16[2048,512]{1,0:T(8,128)(2,1)}, u32[]{:S(2)}) copy-start(bf16[2048,512]{1,0:T(8,128)(2,1)} %param.15) | copy-start | bytes 6291460
  2.2 10.1 %copy-start.8 = (f32[512]{0:T(512)S(1)}, f32[512]{0:T(512)}, u32[]{:S(2)}) copy-start(f32[512]{0:T(512)} %param.16) | copy-start | bytes 6148
  5.5 15.7 %copy-start.7 = (bf16[16,512]{1,0:T(8,128)(2,1)S(1)}, bf16[16,512]{1,0:T(8,128)(2,1)}, u32[]{:S(2)}) copy-start(bf16[16,512]{1,0:T(8,128)(2,1)} %param.21) | copy-start | bytes 49156
  5.5 15.8 %copy-start.5 = (bf16[512,512]{1,0:T(8,128)(2,1)S(1)}, bf16[512,512]{1,0:T(8,128)(2,1)}, u32[]{:S(2)}) copy-start(bf16[512,512]{1,0:T(8,128)(2,1)} %param.17) | copy-start | bytes 1572868
  5.5 253.3 %collective-permute-start.3 = (bf16[2048,512]{0,1:T(8,128)(2,1)S(1)}, bf16[2048,512]{0,1:T(8,128)(2,1)}, u32[]{:S(2)}, u32[]{:S(2)}) collective-permute-start(bf16[2048,512]{0,1:T(8,128)(2,1)S(1)} %convolution_convert_fusion), channel_id=1, source_target_pairs={{0,2},{2,4},{4,6},{6,8},{8,10},{10,12},{12,14},{1,3},{3,5},{5,7},{... | collective-permute-start | bytes 6291464 | tf_op jit(solution)/shard_map/ppermute | solution.py:15
  8.8 255.1 %collective-permute-start.4 = (bf16[2048,512]{0,1:T(8,128)(2,1)S(1)}, bf16[2048,512]{0,1:T(8,128)(2,1)}, u32[]{:S(2)}, u32[]{:S(2)}) collective-permute-start(bf16[2048,512]{0,1:T(8,128)(2,1)S(1)} %convolution_convert_fusion), channel_id=1, source_target_pairs={{2,0},{4,2},{6,4},{8,6},{10,8},{12,10},{14,12},{3,1},{5,3},{7,5},{... | collective-permute-start | bytes 6291464 | tf_op jit(solution)/shard_map/ppermute | solution.py:15
  10.9 252.9 %collective-permute-start.5 = (bf16[2048,512]{0,1:T(8,128)(2,1)S(1)}, bf16[2048,512]{0,1:T(8,128)(2,1)}, u32[]{:S(2)}, u32[]{:S(2)}) collective-permute-start(bf16[2048,512]{0,1:T(8,128)(2,1)S(1)} %convolution_convert_fusion), channel_id=1, source_target_pairs={{0,1},{1,0},{2,3},{3,2},{4,5},{5,4},{6,7},{7,6},{8,9},{9,8},{10,11... | collective-permute-start | bytes 6291464 | tf_op jit(solution)/shard_map/ppermute | solution.py:21
  15.1 7.8 %copy-start.12 = (s32[16]{0:T(128)S(1)}, s32[16]{0:T(128)}, u32[]{:S(2)}) copy-start(s32[16]{0:T(128)} %param.25) | copy-start | bytes 196
  15.1 7.8 %copy-start.10 = (s32[16,4]{0,1:T(4,128)S(1)}, s32[16,4]{0,1:T(4,128)}, u32[]{:S(2)}) copy-start(s32[16,4]{0,1:T(4,128)} %param.24) | copy-start | bytes 772
  15.1 267.2 %collective-permute-start = (bf16[2048,512]{0,1:T(8,128)(2,1)}, bf16[2048,512]{0,1:T(8,128)(2,1)}, u32[]{:S(2)}, u32[]{:S(2)}) collective-permute-start(bf16[2048,512]{0,1:T(8,128)(2,1)} %convolution_convert_fusion.2), channel_id=1, source_target_pairs={{0,2},{2,4},{4,6},{6,8},{8,10},{10,12},{12,14},{1,3},{3,5},{5,7},{... | collective-permute-start | bytes 6291464 | tf_op jit(solution)/shard_map/ppermute | solution.py:15
  19.2 263.1 %collective-permute-start.1 = (bf16[2048,512]{0,1:T(8,128)(2,1)}, bf16[2048,512]{0,1:T(8,128)(2,1)}, u32[]{:S(2)}, u32[]{:S(2)}) collective-permute-start(bf16[2048,512]{0,1:T(8,128)(2,1)} %convolution_convert_fusion.2), channel_id=1, source_target_pairs={{2,0},{4,2},{6,4},{8,6},{10,8},{12,10},{14,12},{3,1},{5,3},{7,5},{... | collective-permute-start | bytes 6291464 | tf_op jit(solution)/shard_map/ppermute | solution.py:15
  30.1 227.3 %copy-start.4 = (bf16[512,512]{1,0:T(8,128)(2,1)S(1)}, bf16[512,512]{1,0:T(8,128)(2,1)}, u32[]{:S(2)}) copy-start(bf16[512,512]{1,0:T(8,128)(2,1)} %param.18) | copy-start | bytes 1572868
  32.9 225.7 %copy-start.9 = (s32[16,6]{0,1:T(8,128)S(1)}, s32[16,6]{0,1:T(8,128)}, u32[]{:S(2)}) copy-start(s32[16,6]{0,1:T(8,128)} %param.22) | copy-start | bytes 1156
  32.9 225.8 %copy-start.11 = (s32[16]{0:T(128)S(1)}, s32[16]{0:T(128)}, u32[]{:S(2)}) copy-start(s32[16]{0:T(128)} %param.23) | copy-start | bytes 196
  201.4 0.7 copy-start.6
  258.8 23.5 %collective-permute-start.2 = (bf16[2048,512]{0,1:T(8,128)(2,1)}, bf16[2048,512]{0,1:T(8,128)(2,1)}, u32[]{:S(2)}, u32[]{:S(2)}) collective-permute-start(bf16[2048,512]{0,1:T(8,128)(2,1)} %convolution_convert_fusion.2), channel_id=1, source_target_pairs={{0,1},{1,0},{2,3},{3,2},{4,5},{5,4},{6,7},{7,6},{8,9},{9,8},{10,11... | collective-permute-start | bytes 6291464 | tf_op jit(solution)/shard_map/ppermute | solution.py:21
  301.2 248.4 %copy-start.3 = (bf16[2048,512]{1,0:T(8,128)(2,1)S(1)}, bf16[2048,512]{1,0:T(8,128)(2,1)}, u32[]{:S(2)}) copy-start(bf16[2048,512]{1,0:T(8,128)(2,1)} %param.15) | copy-start | bytes 6291460
  549.7 4.4 copy-start.1
where the time goes:
time: 562 us; the launch traced here: 554 us
  blocking collectives  203 us (36%)
  local copies, waits for them, and re-layouts  162 us (29%)
  matrix products  120 us (21%)
  other arithmetic  54.5 us (10%)
  starting transfers between devices  13 us (2%)
    all_gather x3, blocking collectives, combined_all(): lax.all_gather(a.astype(kind), axis)  203 us
    dot_general x4, matrix products, group_attention(): jnp.einsum('ghqk,gkhd->gqhd', tile_weights.astype(jnp.bfloat16), tile_val...  43.1 us
    dot_general x4, matrix products, group_attention(): jnp.einsum('gqhd,gkhd->ghqk', query_heads, tile_keys, preferred_element_t...  41.7 us
    reshape x4, local copies, waits for them, and re-layouts, group_attention(): pool_value_blocks[tile_rows]  35.6 us
    reshape x4, local copies, waits for them, and re-layouts, group_attention(): pool_key_blocks[tile_rows]  35.6 us
    reduce_sum x4, other arithmetic, group_attention(): total_sum = jnp.sum(tile_weights, axis=3) + jnp.sum(virt_weights, axis=3)  26.1 us
    while x2, local copies, waits for them, and re-layouts, body(): mixed = lax.map(attend, grouped).reshape(blocks_here * BLOCK, width)  23.9 us
    gather x4, local copies, waits for them, and re-layouts, group_attention(): pool_value_blocks[tile_rows]  23.8 us
  transfers between devices with their start and end apart: 6, of which 0 were waited for; matrix products, arithmetic and copies ran while one was open for 11% of the time, Pallas kernels for 0%

commit v1 on v0

v1 whole, which is shorter than its diff:
```python
import functools
import math

import jax
import jax.numpy as jnp
from jax import lax
from jax.experimental import pallas as pl
from jax.experimental.pallas import tpu as pltpu
from jax.sharding import PartitionSpec as P

HEADS = 8
BLOCK = 128
CHUNK = 256
WINDOW = 8
WINDOW_START = 2
LOG2E = math.log2(math.e)
MESH = pl.DeviceIdType.MESH
F32 = jnp.float32
BF16 = jnp.bfloat16


def dot_nt(a, b):
    return lax.dot_general(a, b, (((1,), (1,)), ((), ())), preferred_element_type=F32)


def normalize(values, gain):
    widened = values.astype(F32)
    mean = jnp.mean(widened * widened, axis=-1, keepdims=True)
    return (widened * lax.rsqrt(mean + 1e-05) * gain).astype(BF16)


def exchange_kernel(
    n_gx,
    n_gy,
    feat,
    gain_ref,
    wq,
    wk,
    wv,
    vquery,
    members,
    counts,
    q_out,
    k_out,
    vt_out,
    vk_out,
    vvt_out,
    own,
    direct,
    far,
    partner,
    q_buf,
    k_buf,
    vt_buf,
    wvt,
    scores,
    packet,
    packets,
    load_sem,
    direct_send,
    direct_recv,
    partner_send,
    partner_recv,
    far_send,
    far_recv,
    packet_send,
    packet_recv,
    q_sem,
    k_sem,
    vt_sem,
):
    rows, width = own.shape
    chunks = rows // CHUNK
    per_chunk = CHUNK // BLOCK
    blocks = rows // BLOCK
    n_dev = n_gx * n_gy
    head = width // HEADS
    scaling = head ** (-0.5)
    gx = lax.axis_index("gx")
    gy = lax.axis_index("gy")
    me = gx * n_gy + gy
    odd = lax.rem(gx, 2)
    beside = gx + 1 - 2 * odd
    onward = gx + 2 - 4 * odd
    origin = gx - 2 + 4 * odd
    has_onward = (onward >= 0) & (onward < n_gx)
    has_origin = (origin >= 0) & (origin < n_gx)
    direct_slot = 2 - odd
    far_slot = 1 + odd

    barrier = pltpu.get_barrier_semaphore()

    def greet(j, carry):
        peer = lax.rem(me + j, n_dev)
        pl.semaphore_signal(
            barrier,
            inc=1,
            device_id={"gx": peer // n_gy, "gy": lax.rem(peer, n_gy)},
            device_id_type=MESH,
        )
        return carry

    lax.fori_loop(1, n_dev, greet, 0)
    pl.semaphore_wait(barrier, n_dev - 1)

    def piece(c):
        return pl.ds(pl.multiple_of(c * CHUNK, CHUNK), CHUNK)

    def direct_copy(c):
        return pltpu.make_async_remote_copy(
            src_ref=feat.at[piece(c)],
            dst_ref=direct.at[piece(c)],
            send_sem=direct_send.at[c],
            recv_sem=direct_recv.at[c],
            device_id={"gx": beside},
            device_id_type=MESH,
        )

    def partner_copy(c):
        return pltpu.make_async_remote_copy(
            src_ref=feat.at[piece(c)],
            dst_ref=partner.at[piece(c)],
            send_sem=partner_send.at[c],
            recv_sem=partner_recv.at[c],
            device_id={"gy": 1 - gy},
            device_id_type=MESH,
        )

    def far_copy(c):
        return pltpu.make_async_remote_copy(
            src_ref=direct.at[piece(c)],
            dst_ref=far.at[piece(c)],
            send_sem=far_send.at[c],
            recv_sem=far_recv.at[c],
            device_id={"gx": onward},
            device_id_type=MESH,
        )

    def packet_copy(peer):
        return pltpu.make_async_remote_copy(
            src_ref=packet,
            dst_ref=packets.at[me],
            send_sem=packet_send,
            recv_sem=packet_recv,
            device_id={"gx": peer // n_gy, "gy": lax.rem(peer, n_gy)},
            device_id_type=MESH,
        )

    def k_copy(slot, c):
        at = pl.ds(slot * blocks + c * per_chunk, per_chunk)
        return pltpu.make_async_copy(k_buf.at[at], k_out.at[at], k_sem.at[slot, c])

    def vt_copy(slot, c):
        at = pl.ds(slot * blocks + c * per_chunk, per_chunk)
        return pltpu.make_async_copy(vt_buf.at[at], vt_out.at[at], vt_sem.at[slot, c])

    def q_copy(c):
        return pltpu.make_async_copy(q_buf.at[piece(c)], q_out.at[piece(c)], q_sem.at[c])

    def start_all(c, carry):
        direct_copy(c).start()
        partner_copy(c).start()
        return carry

    load = pltpu.make_async_copy(feat, own, load_sem)
    load.start()
    lax.fori_loop(0, chunks, start_all, 0)

    gain = gain_ref[...]
    wvt[...] = wv[...].astype(F32).T.astype(BF16)

    @pl.when(jnp.logical_not(has_origin))
    def _():
        far[...] = jnp.zeros_like(far)

    def key_values(source, slot, c):
        normed = normalize(source[piece(c)], gain)
        at = slot * blocks + c * per_chunk
        keys = jnp.dot(normed, wk[...], preferred_element_type=F32).astype(BF16)
        k_buf[pl.ds(at, per_chunk)] = keys.reshape(per_chunk, BLOCK, width)
        values = dot_nt(wvt[...], normed).astype(BF16)
        for i in range(per_chunk):
            vt_buf[at + i] = values[:, i * BLOCK : (i + 1) * BLOCK]
        k_copy(slot, c).start()
        vt_copy(slot, c).start()
        return normed

    load.wait()

    def own_step(c, carry):
        normed = key_values(own, 0, c)
        q_buf[piece(c)] = jnp.dot(normed, wq[...], preferred_element_type=F32).astype(BF16)
        q_copy(c).start()
        return carry

    lax.fori_loop(0, chunks, own_step, 0)

    def forward(c):
        direct_copy(c).wait_recv()

        @pl.when(has_onward)
        def _():
            far_copy(c).start()

    forward(0)

    virt_total = vquery.shape[0]
    virt_normed = normalize(vquery[...], gain)
    virt_q = jnp.dot(virt_normed, wq[...], preferred_element_type=F32).astype(BF16)
    virt_sk = jnp.dot(virt_normed, wk[...], preferred_element_type=F32).astype(BF16)
    virt_sv = jnp.dot(virt_normed, wv[...], preferred_element_type=F32).astype(BF16)

    def node_of(shape):
        offset = lax.broadcasted_iota(jnp.int32, shape, 0)
        return lax.rem(me - WINDOW_START + offset + virt_total, virt_total)

    pick = lax.broadcasted_iota(jnp.int32, (WINDOW, virt_total), 1) == node_of((WINDOW, virt_total))
    window_q = jnp.dot(pick.astype(F32).astype(BF16), virt_q, preferred_element_type=F32)
    row_head = lax.broadcasted_iota(jnp.int32, (HEADS * WINDOW, width), 0) // WINDOW
    column_head = lax.broadcasted_iota(jnp.int32, (HEADS * WINDOW, width), 1) // head
    own_head = row_head == column_head
    spread_q = jnp.where(own_head, jnp.concatenate([window_q] * HEADS, axis=0), 0.0).astype(BF16)
    nodes = node_of((WINDOW, BLOCK))

    def inside(b):
        hit = jnp.zeros((WINDOW, BLOCK), F32)
        for m in range(members.shape[1]):
            used = jnp.where(m < counts[b], members[b, m], -1)
            hit = jnp.where(nodes == used, 1.0, hit)
        return jnp.concatenate([hit] * HEADS, axis=0) > 0.5

    def score_step(b, highest):
        s = jnp.where(inside(b), dot_nt(spread_q, k_buf[b]) * scaling, -1e30)
        scores[b] = s
        return jnp.maximum(highest, s)

    highest = lax.fori_loop(
        0, blocks, score_step, jnp.full((HEADS * WINDOW, BLOCK), -1e30, F32)
    )
    local_max = jnp.max(highest, axis=1, keepdims=True)

    def weight_step(b, carry):
        total, numer = carry
        w = jnp.where(inside(b), jnp.exp(scores[b] - local_max), 0.0)
        high = w.astype(BF16)
        low = (w - high.astype(F32)).astype(BF16)
        both = dot_nt(jnp.concatenate([high, low], axis=0), vt_buf[b])
        numer = numer + both[: HEADS * WINDOW] + both[HEADS * WINDOW :]
        return total + w, numer

    total, numer = lax.fori_loop(
        0,
        blocks,
        weight_step,
        (
            jnp.zeros((HEADS * WINDOW, BLOCK), F32),
            jnp.zeros((HEADS * WINDOW, width), F32),
        ),
    )
    total = jnp.sum(total, axis=1, keepdims=True)
    numer = jnp.where(own_head, numer, 0.0)
    lane = lax.broadcasted_iota(jnp.int32, (WINDOW, BLOCK), 1)
    packed_max = jnp.zeros((WINDOW, BLOCK), F32)
    packed_total = jnp.zeros((WINDOW, BLOCK), F32)
    packed_numer = jnp.zeros((WINDOW, width), F32)
    for h in range(HEADS):
        at = slice(h * WINDOW, (h + 1) * WINDOW)
        packed_max = jnp.where(lane == h, local_max[at], packed_max)
        packed_total = jnp.where(lane == h, total[at], packed_total)
        packed_numer = packed_numer + numer[at]
    packet[...] = jnp.concatenate([packed_numer, packed_max, packed_total], axis=1)
    packets[me] = packet[...]

    def send_packet(j, carry):
        packet_copy(lax.rem(me + j, n_dev)).start()
        return carry

    lax.fori_loop(1, n_dev, send_packet, 0)

    def far_step(c):
        @pl.when(has_origin)
        def _():
            far_copy(c).wait_recv()

        key_values(far, far_slot, c)

    def near_step(c, carry):
        @pl.when(c > 0)
        def _():
            forward(c)

        partner_copy(c).wait_recv()
        key_values(direct, direct_slot, c)
        key_values(partner, 3, c)

        @pl.when(c >= 2)
        def _():
            far_step(c - 2)

        return carry

    half = chunks // 2
    lax.fori_loop(0, half, near_step, 0)

    others = packets.at[pl.ds(0, n_dev - 1)]
    pltpu.make_async_copy(others, others, packet_recv).wait()
    pltpu.make_async_copy(others, others, packet_send).wait()
    head_lane = (
        lax.broadcasted_iota(jnp.int32, (BLOCK, width), 0)
        == lax.broadcasted_iota(jnp.int32, (BLOCK, width), 1) // head
    ).astype(F32)

    def widen(x):
        return jnp.dot(x, head_lane, precision=lax.Precision.HIGHEST, preferred_element_type=F32)

    products = virt_q.astype(F32) * virt_sk.astype(F32)
    self_score = (
        lax.dot_general(
            products,
            head_lane,
            (((1,), (1,)), ((), ())),
            precision=lax.Precision.HIGHEST,
            preferred_element_type=F32,
        )
        * scaling
    )
    parts = []
    for k in range(WINDOW):
        part = packets[:, k, :]
        shift = (WINDOW_START - k) % n_dev
        if shift:
            part = jnp.concatenate([part[shift:], part[:shift]], axis=0)
        parts.append(part)
    top = self_score
    for part in parts:
        top = jnp.maximum(top, part[:, width : width + BLOCK])
    self_weight = jnp.exp(self_score - top)
    joined_total = self_weight
    joined = widen(self_weight) * virt_sv.astype(F32)
    for part in parts:
        scale = jnp.exp(part[:, width : width + BLOCK] - top)
        joined_total = joined_total + scale * part[:, width + BLOCK :]
        joined = joined + widen(scale) * part[:, :width]
    aggregate = (joined / widen(joined_total)).astype(BF16)
    vk_out[...] = jnp.dot(aggregate, wk[...], preferred_element_type=F32).astype(BF16)
    vvt_out[...] = dot_nt(wvt[...], aggregate).astype(BF16)

    lax.fori_loop(half, chunks, near_step, 0)
    far_step(chunks - 2)
    far_step(chunks - 1)

    def finish(c, carry):
        direct_copy(c).wait_send()
        partner_copy(c).wait_send()

        @pl.when(has_onward)
        def _():
            far_copy(c).wait_send()

        q_copy(c).wait()
        for slot in range(4):
            k_copy(slot, c).wait()
            vt_copy(slot, c).wait()
        return carry

    lax.fori_loop(0, chunks, finish, 0)


def attention_kernel(slots, tiles, counts, *refs):
    q_ref, feat_ref = refs[:2]
    k_refs = refs[2 : 2 + slots]
    vt_refs = refs[2 + slots : 2 + 2 * slots]
    vk_ref, vvt_ref, wo_ref, out_ref, mixed_ref = refs[2 + 2 * slots :]
    b = pl.program_id(0)
    count = counts[b]
    width = q_ref.shape[1]
    head = width // HEADS
    factor = head ** (-0.5) * LOG2E
    pair = 2 * head

    def attend(masked):
        for e in range(HEADS // 2):
            columns = slice(e * pair, (e + 1) * pair)
            q = q_ref[:, columns]
            first = lax.broadcasted_iota(jnp.int32, q.shape, 1) < head
            zero = jnp.zeros_like(q)
            both = jnp.concatenate([jnp.where(first, q, zero), jnp.where(first, zero, q)], axis=0)
            virt_s = dot_nt(vk_ref[:, columns], both)
            tile_s = []
            for i in range(slots):
                s = dot_nt(k_refs[i][0, :, columns], both)
                if masked and i:
                    s = s + jnp.where(i < count, 0.0, -1e30)
                tile_s.append(s)
            top = jnp.max(virt_s, axis=0, keepdims=True)
            for s in tile_s:
                top = jnp.maximum(top, jnp.max(s, axis=0, keepdims=True))
            tile_w = jnp.concatenate(
                [jnp.exp2((s - top) * factor).astype(BF16) for s in tile_s], axis=0
            )
            virt_w = jnp.exp2((virt_s - top) * factor).astype(BF16)
            tile_v = jnp.concatenate([r[0, columns, :] for r in vt_refs], axis=1)
            tile_v = jnp.concatenate([tile_v, jnp.ones((16, tile_v.shape[1]), BF16)], axis=0)
            virt_v = vvt_ref[columns, :]
            virt_v = jnp.concatenate([virt_v, jnp.ones((16, virt_v.shape[1]), BF16)], axis=0)
            sums = jnp.dot(tile_v, tile_w, preferred_element_type=F32) + jnp.dot(
                virt_v, virt_w, preferred_element_type=F32
            )
            scale = 1.0 / sums[pair : pair + 1]
            mixed = jnp.concatenate(
                [
                    sums[:head, :BLOCK] * scale[:, :BLOCK],
                    sums[head:pair, BLOCK:] * scale[:, BLOCK:],
                ],
                axis=0,
            )
            mixed_ref[:, columns] = mixed.T.astype(BF16)

    @pl.when(count == slots)
    def _():
        attend(False)

    @pl.when(count < slots)
    def _():
        attend(True)

    out_ref[...] = (
        feat_ref[...].astype(F32)
        + jnp.dot(mixed_ref[...], wo_ref[...], preferred_element_type=F32)
    ).astype(BF16)


def body(
    n_gx,
    n_gy,
    features,
    norm_gain,
    query_weight,
    key_weight,
    value_weight,
    output_weight,
    virtual_query,
    tile_list,
    tile_count,
    member_list,
    member_count,
):
    rows, width = features.shape
    blocks = rows // BLOCK
    chunks = rows // CHUNK
    n_dev = n_gx * n_gy
    virt_total = virtual_query.shape[0]
    slots = tile_list.shape[1]
    assert virt_total == n_dev and n_gx % 2 == 0 and n_gy == 2
    vmem = pl.BlockSpec(memory_space=pltpu.VMEM)
    smem = pl.BlockSpec(memory_space=pltpu.SMEM)
    hbm = pl.BlockSpec(memory_space=pl.ANY)
    dma = pltpu.SemaphoreType.DMA
    packet_width = width + 2 * BLOCK
    queries, keys, values_t, virt_keys, virt_values_t = pl.pallas_call(
        functools.partial(exchange_kernel, n_gx, n_gy),
        out_shape=[
            jax.ShapeDtypeStruct((rows, width), BF16),
            jax.ShapeDtypeStruct((4 * blocks, BLOCK, width), BF16),
            jax.ShapeDtypeStruct((4 * blocks, width, BLOCK), BF16),
            jax.ShapeDtypeStruct((virt_total, width), BF16),
            jax.ShapeDtypeStruct((width, virt_total), BF16),
        ],
        in_specs=[hbm, vmem, vmem, vmem, vmem, vmem, smem, smem],
        out_specs=[hbm, hbm, hbm, vmem, vmem],
        scratch_shapes=[pltpu.VMEM((rows, width), BF16)] * 5
        + [
            pltpu.VMEM((4 * blocks, BLOCK, width), BF16),
            pltpu.VMEM((4 * blocks, width, BLOCK), BF16),
            pltpu.VMEM((width, width), BF16),
            pltpu.VMEM((blocks, HEADS * WINDOW, BLOCK), F32),
            pltpu.VMEM((WINDOW, packet_width), F32),
            pltpu.VMEM((n_dev, WINDOW, packet_width), F32),
            dma,
            dma((chunks,)),
            dma((chunks,)),
            dma((chunks,)),
            dma((chunks,)),
            dma((chunks,)),
            dma((chunks,)),
            dma,
            dma,
            dma((chunks,)),
            dma((4, chunks)),
            dma((4, chunks)),
        ],
        compiler_params=pltpu.CompilerParams(
            collective_id=0, has_side_effects=True, vmem_limit_bytes=56 * 1024 * 1024
        ),
        name="exchange",
    )(
        features,
        norm_gain.reshape(1, width),
        query_weight,
        key_weight,
        value_weight,
        virtual_query,
        member_list,
        member_count,
    )

    def tile_at(i):
        return lambda b, tiles, counts: (
            jnp.where(i < counts[b], tiles[b, i], tiles[b, 0]),
            0,
            0,
        )

    row_spec = pl.BlockSpec((BLOCK, width), lambda b, *_: (b, 0))
    whole = lambda shape: pl.BlockSpec(shape, lambda b, *_: (0, 0))
    return pl.pallas_call(
        functools.partial(attention_kernel, slots),
        out_shape=jax.ShapeDtypeStruct((rows, width), BF16),
        grid_spec=pltpu.PrefetchScalarGridSpec(
            num_scalar_prefetch=2,
            grid=(blocks,),
            in_specs=[row_spec, row_spec]
            + [pl.BlockSpec((1, BLOCK, width), tile_at(i)) for i in range(slots)]
            + [pl.BlockSpec((1, width, BLOCK), tile_at(i)) for i in range(slots)]
            + [
                whole((virt_total, width)),
                whole((width, virt_total)),
                whole((width, width)),
            ],
            out_specs=row_spec,
            scratch_shapes=[pltpu.VMEM((BLOCK, width), BF16)],
        ),
        compiler_params=pltpu.CompilerParams(vmem_limit_bytes=48 * 1024 * 1024),
        name="attention",
    )(
        tile_list,
        tile_count,
        queries,
        features,
        *[keys] * slots,
        *[values_t] * slots,
        virt_keys,
        virt_values_t,
        output_weight,
    )


def solution(mesh):
    split = ("groups", "gx", "gy")
    placed = (P(split, None),) + (P(),) * 6 + (P(split, None), P(split), P(split, None), P(split))
    return jax.shard_map(
        functools.partial(body, mesh.shape["gx"], mesh.shape["gy"]),
        mesh=mesh,
        in_specs=placed,
        out_specs=P(split, None),
        check_vma=False,
    )
```

time: 562 us -> 136 us (0.24); the launches traced: 554 us -> 134 us
  blocking collectives: 203 us -> 0 us
  local copies, waits for them, and re-layouts: 162 us -> 5.48 us
  Pallas kernels: 0 us -> 128 us
  matrix products: 120 us -> 0 us
  other arithmetic: 54.5 us -> 0 us
  starting transfers between devices: 13 us -> 0 us
    all_gather x3 -> x0, blocking collectives: 203 us -> none  [combined_all(): lax.all_gather(a.astype(kind), axis)]
    pallas_call x0 -> x2, Pallas kernels: none -> 128 us  [the longest x1 84.3 us: body(): pl.pallas_call(functools.partial(exchange_kernel, n_gx, n_gy), out_shape=...]
    dot_general x41 -> x0, matrix products: 120 us -> none  [the longest x4 43.1 us: group_attention(): jnp.einsum('ghqk,gkhd->gqhd', tile_weights.astype(jnp.bfloat16), tile_val...]
    reshape x18 -> x0, local copies, waits for them, and re-layouts: 72 us -> none  [the longest x4 35.6 us: group_attention(): pool_value_blocks[tile_rows]]
    gather x8 -> x0, local copies, waits for them, and re-layouts: 47.5 us -> none  [the longest x4 23.8 us: group_attention(): pool_value_blocks[tile_rows]]
    reduce_sum x8 -> x0, other arithmetic: 28.9 us -> none  [the longest x4 26.1 us: group_attention(): total_sum = jnp.sum(tile_weights, axis=3) + jnp.sum(virt_weights, axis=3)]
    while x2 -> x0, local copies, waits for them, and re-layouts: 23.9 us -> none  [body(): mixed = lax.map(attend, grouped).reshape(blocks_here * BLOCK, width)]
    concatenate x2 -> x0, other arithmetic: 13.5 us -> none  [the longest x1 7.01 us: body(): jnp.concatenate([values_own, lower_values, upper_values, partner_values],...]
  transfers between devices with their start and end apart: 6 -> 0, of which waited for: 0 -> 0; matrix products, arithmetic and copies ran while one was open for 11% -> 0% of each run, Pallas kernels for 0% -> 0%
where the time goes in v1:
time: 136 us; the launch traced here: 134 us
  Pallas kernels  128 us (94%)
  local copies, waits for them, and re-layouts  5.48 us (4%)
    pallas_call x1, Pallas kernels, body(): pl.pallas_call(functools.partial(exchange_kernel, n_gx, n_gy), out_shape=...  84.3 us
    pallas_call x1, Pallas kernels, body(): pl.pallas_call(functools.partial(attention_kernel, slots), out_shape=jax....  44 us
    unnamed x14, local copies, waits for them, and re-layouts  5.48 us

profile of v1, /device:TPU:13, one launch (start us, length us, event | category | flops | bytes accessed | tf_op | source)
XLA Modules:
  0.0 133.8 jit_solution(9471170755408929841)
XLA Ops:
  0.0 0.0 copy-start
  0.0 0.0 copy-start.5
  0.0 0.0 copy-start.2
  0.0 0.9 copy.13.tiles
  0.9 1.4 %copy.12.members = s32[16,4]{1,0:T(8,128)} copy(s32[16,4]{0,1:T(4,128)} %param.20) | data formatting | bytes 512 | tf_op args[9]
  2.3 84.3 %exchange.1 = (bf16[2048,512]{1,0:T(8,128)(2,1)}, bf16[64,128,512]{2,1,0:T(8,128)(2,1)}, bf16[64,512,128]{2,1,0:T(8,128)(2,1)}, bf16[16,512]{1,0:T(8,128)(2,1)}, bf16[512,16]{1,0:T(8,128)(2,1)}) custom-call(bf16[2048,512]{1,0:T(8,128)(2,1)} %refs_1_.1, f32[1,512]{1,0:T(1,128)} %bitcast.1, bf16[512,512]{1,0:T(8,128)(2,1)} %wq.1, bf16[512,512]{1,0:T(8,128)(2,1)} %wk.1, ...), custom_call_target="tpu_custom_call" | custom-call | tf_op jit(solution)/shard_map/exchange/pallas_call | solution.py:460
  86.6 0.0 copy-done
  86.6 0.0 copy-done.5
  86.6 0.0 copy-done.2
  86.6 0.0 copy-start.1
  86.6 1.6 %copy-done.1 = bf16[2048,512]{1,0:T(8,128)(2,1)S(1)} copy-done((bf16[2048,512]{1,0:T(8,128)(2,1)S(1)}, bf16[2048,512]{1,0:T(8,128)(2,1)}, u32[]{:S(2)}) %copy-start.1) | copy-done | bytes 2097176
  88.2 0.0 copy-start.3
  88.2 0.9 copy-done.3
  89.1 0.0 copy-start.4
  89.1 0.7 copy-done.4
  89.8 44.0 %attention.1 = bf16[2048,512]{1,0:T(8,128)(2,1)} custom-call(s32[16,6]{1,0:T(8,128)S(1)} %copy.13.tiles, s32[16]{0:T(128)S(1)} %copy-done.5, bf16[2048,512]{1,0:T(8,128)(2,1)S(1)} %copy-done.1, bf16[2048,512]{1,0:T(8,128)(2,1)S(1)} %copy-done, bf16[64,128,512]{2,1,0:T(8,128)(2,1)} %get-tuple-element.11.refs_2_.refs_3_.refs_4_.refs_5_.refs_6_.refs_7_, ...), custom_call_target="tpu_custom_call" | custom-call | tf_op jit(solution)/shard_map/attention/pallas_call | solution.py:516
Async XLA Ops:
  0.0 86.6 %copy-start = (bf16[2048,512]{1,0:T(8,128)(2,1)S(1)}, bf16[2048,512]{1,0:T(8,128)(2,1)}, u32[]{:S(2)}) copy-start(bf16[2048,512]{1,0:T(8,128)(2,1)} %refs_1_.1) | copy-start | bytes 6291460
  0.0 86.6 %copy-start.5 = (s32[16]{0:T(128)S(1)}, s32[16]{0:T(128)}, u32[]{:S(2)}) copy-start(s32[16]{0:T(128)} %counts.3) | copy-start | bytes 196
  0.0 86.6 %copy-start.2 = (bf16[512,512]{1,0:T(8,128)(2,1)S(1)}, bf16[512,512]{1,0:T(8,128)(2,1)}, u32[]{:S(2)}) copy-start(bf16[512,512]{1,0:T(8,128)(2,1)} %refs_16_.1) | copy-start | bytes 1572868
  86.6 1.6 %copy-start.1 = (bf16[2048,512]{1,0:T(8,128)(2,1)S(1)}, bf16[2048,512]{1,0:T(8,128)(2,1)}, u32[]{:S(2)}) copy-start(bf16[2048,512]{1,0:T(8,128)(2,1)} %get-tuple-element.10.refs_0_) | copy-start | bytes 6291460
  88.2 0.9 copy-start.3
  89.1 0.7 copy-start.4

commit v2 on v1

--- a/solution.py
+++ b/solution.py
@@ -11,6 +11,8 @@
 HEADS = 8
 BLOCK = 128
 CHUNK = 256
+SEND = 128
+DEPTH = 3
 WINDOW = 8
 WINDOW_START = 2
 LOG2E = math.log2(math.e)
@@ -71,6 +73,7 @@
 ):
     rows, width = own.shape
     chunks = rows // CHUNK
+    sends = rows // SEND
     per_chunk = CHUNK // BLOCK
     blocks = rows // BLOCK
     n_dev = n_gx * n_gy
@@ -106,10 +109,13 @@
     def piece(c):
         return pl.ds(pl.multiple_of(c * CHUNK, CHUNK), CHUNK)
 
+    def span(c):
+        return pl.ds(pl.multiple_of(c * SEND, SEND), SEND)
+
     def direct_copy(c):
         return pltpu.make_async_remote_copy(
-            src_ref=feat.at[piece(c)],
-            dst_ref=direct.at[piece(c)],
+            src_ref=feat.at[span(c)],
+            dst_ref=direct.at[span(c)],
             send_sem=direct_send.at[c],
             recv_sem=direct_recv.at[c],
             device_id={"gx": beside},
@@ -128,8 +134,8 @@
 
     def far_copy(c):
         return pltpu.make_async_remote_copy(
-            src_ref=direct.at[piece(c)],
-            dst_ref=far.at[piece(c)],
+            src_ref=direct.at[span(c)],
+            dst_ref=far.at[span(c)],
             send_sem=far_send.at[c],
             recv_sem=far_recv.at[c],
             device_id={"gx": onward},
@@ -157,14 +163,15 @@
     def q_copy(c):
         return pltpu.make_async_copy(q_buf.at[piece(c)], q_out.at[piece(c)], q_sem.at[c])
 
-    def start_all(c, carry):
+    def start_partner(c, carry):
+        partner_copy(c).start()
+        return carry
+
+    for c in range(DEPTH):
         direct_copy(c).start()
-        partner_copy(c).start()
-        return carry
-
     load = pltpu.make_async_copy(feat, own, load_sem)
     load.start()
-    lax.fori_loop(0, chunks, start_all, 0)
+    lax.fori_loop(0, chunks, start_partner, 0)
 
     gain = gain_ref[...]
     wvt[...] = wv[...].astype(F32).T.astype(BF16)
@@ -193,16 +200,25 @@
         q_copy(c).start()
         return carry
 
-    lax.fori_loop(0, chunks, own_step, 0)
-
-    def forward(c):
+    def service(c):
+        direct_copy(c).wait_send()
+
+        @pl.when(c + DEPTH < sends)
+        def _():
+            direct_copy(c + DEPTH).start()
+
         direct_copy(c).wait_recv()
 
         @pl.when(has_onward)
         def _():
             far_copy(c).start()
 
-    forward(0)
+    lax.fori_loop(0, 4, own_step, 0)
+    service(0)
+    lax.fori_loop(4, 6, own_step, 0)
+    service(1)
+    lax.fori_loop(6, chunks, own_step, 0)
+    service(2)
 
     virt_total = vquery.shape[0]
     virt_normed = normalize(vquery[...], gain)
@@ -238,6 +254,7 @@
         0, blocks, score_step, jnp.full((HEADS * WINDOW, BLOCK), -1e30, F32)
     )
     local_max = jnp.max(highest, axis=1, keepdims=True)
+    service(3)
 
     def weight_step(b, carry):
         total, numer = carry
@@ -280,27 +297,36 @@
     def far_step(c):
         @pl.when(has_origin)
         def _():
-            far_copy(c).wait_recv()
+            for i in range(CHUNK // SEND):
+                far_copy(c * (CHUNK // SEND) + i).wait_recv()
 
         key_values(far, far_slot, c)
 
-    def near_step(c, carry):
-        @pl.when(c > 0)
+    service(4)
+
+    def near_step(j, carry):
+        service(5 + j)
+        partner_copy(j).wait_recv()
+        key_values(partner, 3, j)
+
+        @pl.when(j <= 4)
         def _():
-            forward(c)
-
-        partner_copy(c).wait_recv()
-        key_values(direct, direct_slot, c)
-        key_values(partner, 3, c)
-
-        @pl.when(c >= 2)
+            key_values(direct, direct_slot, j)
+
+        @pl.when(j >= 3)
         def _():
-            far_step(c - 2)
-
-        return carry
-
-    half = chunks // 2
-    lax.fori_loop(0, half, near_step, 0)
+            far_step(j - 3)
+
+        return carry
+
+    lax.fori_loop(0, chunks, near_step, 0)
+
+    def late_step(j, carry):
+        service(8 + j)
+        key_values(direct, direct_slot, j)
+        return carry
+
+    lax.fori_loop(5, chunks, late_step, 0)
 
     others = packets.at[pl.ds(0, n_dev - 1)]
     pltpu.make_async_copy(others, others, packet_recv).wait()
@@ -345,17 +371,16 @@
     vk_out[...] = jnp.dot(aggregate, wk[...], preferred_element_type=F32).astype(BF16)
     vvt_out[...] = dot_nt(wvt[...], aggregate).astype(BF16)
 
-    lax.fori_loop(half, chunks, near_step, 0)
-    far_step(chunks - 2)
-    far_step(chunks - 1)
+    for c in range(5, chunks):
+        far_step(c)
+
+    @pl.when(has_onward)
+    def _():
+        for c in range(sends):
+            far_copy(c).wait_send()
 
     def finish(c, carry):
-        direct_copy(c).wait_send()
         partner_copy(c).wait_send()
-
-        @pl.when(has_onward)
-        def _():
-            far_copy(c).wait_send()
 
         q_copy(c).wait()
         for slot in range(4):
@@ -375,46 +400,46 @@
     count = counts[b]
     width = q_ref.shape[1]
     head = width // HEADS
-    factor = head ** (-0.5) * LOG2E
+    scaling = head ** (-0.5)
     pair = 2 * head
 
     def attend(masked):
-        for e in range(HEADS // 2):
+        first = lax.broadcasted_iota(jnp.int32, (BLOCK, pair), 1) < head
+
+        def score(e):
             columns = slice(e * pair, (e + 1) * pair)
-            q = q_ref[:, columns]
-            first = lax.broadcasted_iota(jnp.int32, q.shape, 1) < head
+            q = q_ref[:, columns] * scaling
             zero = jnp.zeros_like(q)
             both = jnp.concatenate([jnp.where(first, q, zero), jnp.where(first, zero, q)], axis=0)
-            virt_s = dot_nt(vk_ref[:, columns], both)
-            tile_s = []
-            for i in range(slots):
-                s = dot_nt(k_refs[i][0, :, columns], both)
-                if masked and i:
-                    s = s + jnp.where(i < count, 0.0, -1e30)
-                tile_s.append(s)
-            top = jnp.max(virt_s, axis=0, keepdims=True)
-            for s in tile_s:
-                top = jnp.maximum(top, jnp.max(s, axis=0, keepdims=True))
-            tile_w = jnp.concatenate(
-                [jnp.exp2((s - top) * factor).astype(BF16) for s in tile_s], axis=0
-            )
-            virt_w = jnp.exp2((virt_s - top) * factor).astype(BF16)
-            tile_v = jnp.concatenate([r[0, columns, :] for r in vt_refs], axis=1)
-            tile_v = jnp.concatenate([tile_v, jnp.ones((16, tile_v.shape[1]), BF16)], axis=0)
-            virt_v = vvt_ref[columns, :]
-            virt_v = jnp.concatenate([virt_v, jnp.ones((16, virt_v.shape[1]), BF16)], axis=0)
-            sums = jnp.dot(tile_v, tile_w, preferred_element_type=F32) + jnp.dot(
-                virt_v, virt_w, preferred_element_type=F32
-            )
-            scale = 1.0 / sums[pair : pair + 1]
-            mixed = jnp.concatenate(
-                [
-                    sums[:head, :BLOCK] * scale[:, :BLOCK],
-                    sums[head:pair, BLOCK:] * scale[:, BLOCK:],
-                ],
-                axis=0,
-            )
-            mixed_ref[:, columns] = mixed.T.astype(BF16)
+            keys = jnp.concatenate([r[0, :, columns] for r in k_refs] + [vk_ref[:, columns]], axis=0)
+            s = dot_nt(both, keys)
+            if masked:
+                slot = lax.broadcasted_iota(jnp.int32, (1, s.shape[1]), 1) // BLOCK
+                s = s + jnp.where((slot < count) | (slot == slots), 0.0, -1e30)
+            return s
+
+        def mix(e, s):
+            top = jnp.max(s, axis=1, keepdims=True)
+            return jnp.exp(s - top).astype(BF16)
+
+        def close(e, w):
+            columns = slice(e * pair, (e + 1) * pair)
+            v = jnp.concatenate([r[0, columns, :] for r in vt_refs] + [vvt_ref[columns, :]], axis=1)
+            v = jnp.concatenate([v, jnp.ones((128, v.shape[1]), BF16)], axis=0)
+            sums = dot_nt(w, v)
+            sums = sums[:, :pair] / sums[:, pair:]
+            mixed_ref[:, columns] = jnp.where(first, sums[:BLOCK], sums[BLOCK:]).astype(BF16)
+
+        n = HEADS // 2
+        s = score(0)
+        w = None
+        for e in range(n):
+            after = score(e + 1) if e + 1 < n else None
+            if e:
+                close(e - 1, w)
+            w = mix(e, s)
+            s = after
+        close(n - 1, w)
 
     @pl.when(count == slots)
     def _():
@@ -448,10 +473,12 @@
     rows, width = features.shape
     blocks = rows // BLOCK
     chunks = rows // CHUNK
+    sends = rows // SEND
     n_dev = n_gx * n_gy
     virt_total = virtual_query.shape[0]
     slots = tile_list.shape[1]
     assert virt_total == n_dev and n_gx % 2 == 0 and n_gy == 2
+    assert chunks == 8 and sends == 16
     vmem = pl.BlockSpec(memory_space=pltpu.VMEM)
     smem = pl.BlockSpec(memory_space=pltpu.SMEM)
     hbm = pl.BlockSpec(memory_space=pl.ANY)
@@ -477,12 +504,12 @@
             pltpu.VMEM((WINDOW, packet_width), F32),
             pltpu.VMEM((n_dev, WINDOW, packet_width), F32),
             dma,
+            dma((sends,)),
+            dma((sends,)),
             dma((chunks,)),
             dma((chunks,)),
-            dma((chunks,)),
-            dma((chunks,)),
-            dma((chunks,)),
-            dma((chunks,)),
+            dma((sends,)),
+            dma((sends,)),
             dma,
             dma,
             dma((chunks,)),

time: 136 us -> 110 us (0.81); the launches traced: 134 us -> 110 us
  Pallas kernels: 128 us -> 104 us
    pallas_call x1, Pallas kernels: 84.3 us -> 68.4 us  [body(): pl.pallas_call(functools.partial(exchange_kernel, n_gx, n_gy), out_shape=...]
    pallas_call x1, Pallas kernels: 44 us -> 35.7 us  [body(): pl.pallas_call(functools.partial(attention_kernel, slots), out_shape=jax....]
where the time goes in v2:
time: 110 us
  Pallas kernels  104 us (95%)
  local copies, waits for them, and re-layouts  5.48 us (5%)
    pallas_call x1, Pallas kernels, body(): pl.pallas_call(functools.partial(exchange_kernel, n_gx, n_gy), out_shape=...  68.4 us
    pallas_call x1, Pallas kernels, body(): pl.pallas_call(functools.partial(attention_kernel, slots), out_shape=jax....  35.7 us
    unnamed x14, local copies, waits for them, and re-layouts  5.48 us

profile of v2, /device:TPU:13, one launch (start us, length us, event | category | flops | bytes accessed | tf_op | source)
XLA Modules:
  0.0 109.7 jit_solution(7501300620768354876)
XLA Ops:
  0.0 0.0 copy-start
  0.0 0.0 copy-start.5
  0.0 0.0 copy-start.2
  0.0 0.9 copy.13.tiles
  0.9 1.4 %copy.12.members = s32[16,4]{1,0:T(8,128)} copy(s32[16,4]{0,1:T(4,128)} %param.20) | data formatting | bytes 512 | tf_op args[9]
  2.3 68.4 %exchange.1 = (bf16[2048,512]{1,0:T(8,128)(2,1)}, bf16[64,128,512]{2,1,0:T(8,128)(2,1)}, bf16[64,512,128]{2,1,0:T(8,128)(2,1)}, bf16[16,512]{1,0:T(8,128)(2,1)}, bf16[512,16]{1,0:T(8,128)(2,1)}) custom-call(bf16[2048,512]{1,0:T(8,128)(2,1)} %refs_1_.1, f32[1,512]{1,0:T(1,128)} %bitcast.1, bf16[512,512]{1,0:T(8,128)(2,1)} %wq.1, bf16[512,512]{1,0:T(8,128)(2,1)} %wk.1, ...), custom_call_target="tpu_custom_call" | custom-call | tf_op jit(solution)/shard_map/exchange/pallas_call | solution.py:487
  70.7 0.0 copy-done
  70.7 0.0 copy-done.5
  70.7 0.0 copy-done.2
  70.7 0.0 copy-start.1
  70.8 1.6 %copy-done.1 = bf16[2048,512]{1,0:T(8,128)(2,1)S(1)} copy-done((bf16[2048,512]{1,0:T(8,128)(2,1)S(1)}, bf16[2048,512]{1,0:T(8,128)(2,1)}, u32[]{:S(2)}) %copy-start.1) | copy-done | bytes 2097176
  72.3 0.0 copy-start.3
  72.3 0.9 copy-done.3
  73.2 0.0 copy-start.4
  73.2 0.7 copy-done.4
  74.0 35.7 %attention.1 = bf16[2048,512]{1,0:T(8,128)(2,1)} custom-call(s32[16,6]{1,0:T(8,128)S(1)} %copy.13.tiles, s32[16]{0:T(128)S(1)} %copy-done.5, bf16[2048,512]{1,0:T(8,128)(2,1)S(1)} %copy-done.1, bf16[2048,512]{1,0:T(8,128)(2,1)S(1)} %copy-done, bf16[64,128,512]{2,1,0:T(8,128)(2,1)} %get-tuple-element.11.refs_2_.refs_3_.refs_4_.refs_5_.refs_6_.refs_7_, ...), custom_call_target="tpu_custom_call" | custom-call | tf_op jit(solution)/shard_map/attention/pallas_call | solution.py:543
Async XLA Ops:
  0.0 70.7 %copy-start = (bf16[2048,512]{1,0:T(8,128)(2,1)S(1)}, bf16[2048,512]{1,0:T(8,128)(2,1)}, u32[]{:S(2)}) copy-start(bf16[2048,512]{1,0:T(8,128)(2,1)} %refs_1_.1) | copy-start | bytes 6291460
  0.0 70.7 %copy-start.5 = (s32[16]{0:T(128)S(1)}, s32[16]{0:T(128)}, u32[]{:S(2)}) copy-start(s32[16]{0:T(128)} %counts.3) | copy-start | bytes 196
  0.0 70.7 %copy-start.2 = (bf16[512,512]{1,0:T(8,128)(2,1)S(1)}, bf16[512,512]{1,0:T(8,128)(2,1)}, u32[]{:S(2)}) copy-start(bf16[512,512]{1,0:T(8,128)(2,1)} %refs_16_.1) | copy-start | bytes 1572868
  70.7 1.6 %copy-start.1 = (bf16[2048,512]{1,0:T(8,128)(2,1)S(1)}, bf16[2048,512]{1,0:T(8,128)(2,1)}, u32[]{:S(2)}) copy-start(bf16[2048,512]{1,0:T(8,128)(2,1)} %get-tuple-element.10.refs_0_) | copy-start | bytes 6291460
  72.3 0.9 copy-start.3
  73.2 0.7 copy-start.4

commit v3 on v2

--- a/solution.py
+++ b/solution.py
@@ -240,8 +240,8 @@
 
     def inside(b):
         hit = jnp.zeros((WINDOW, BLOCK), F32)
-        for m in range(members.shape[1]):
-            used = jnp.where(m < counts[b], members[b, m], -1)
+        for m in range(members.shape[0]):
+            used = jnp.where(m < counts[b], members[m, b], -1)
             hit = jnp.where(nodes == used, 1.0, hit)
         return jnp.concatenate([hit] * HEADS, axis=0) > 0.5
 
@@ -527,13 +527,13 @@
         key_weight,
         value_weight,
         virtual_query,
-        member_list,
+        member_list.T,
         member_count,
     )
 
     def tile_at(i):
         return lambda b, tiles, counts: (
-            jnp.where(i < counts[b], tiles[b, i], tiles[b, 0]),
+            jnp.where(i < counts[b], tiles[i, b], tiles[0, b]),
             0,
             0,
         )
@@ -557,10 +557,10 @@
             out_specs=row_spec,
             scratch_shapes=[pltpu.VMEM((BLOCK, width), BF16)],
         ),
-        compiler_params=pltpu.CompilerParams(vmem_limit_bytes=48 * 1024 * 1024),
+        compiler_params=pltpu.CompilerParams(vmem_limit_bytes=60 * 1024 * 1024),
         name="attention",
     )(
-        tile_list,
+        tile_list.T,
         tile_count,
         queries,
         features,

time: 110 us -> 106 us (0.964)
  local copies, waits for them, and re-layouts: 5.48 us -> 0 us
    unnamed x14 -> x0, local copies, waits for them, and re-layouts: 5.48 us -> none
    pallas_call x1, Pallas kernels: 35.7 us -> 36.9 us  [body(): pl.pallas_call(functools.partial(attention_kernel, slots), out_shape=jax....]
where the time goes in v3:
time: 106 us; the launch traced here: 105 us
  Pallas kernels  105 us (99%)
    pallas_call x1, Pallas kernels, body(): pl.pallas_call(functools.partial(exchange_kernel, n_gx, n_gy), out_shape=...  68.5 us
    pallas_call x1, Pallas kernels, body(): pl.pallas_call(functools.partial(attention_kernel, slots), out_shape=jax....  36.9 us

profile of v3, /device:TPU:13, one launch (start us, length us, event | category | flops | bytes accessed | tf_op | source)
XLA Modules:
  0.0 105.3 jit_solution(8765144135900732214)
XLA Ops:
  0.0 68.5 %exchange.1 = (bf16[2048,512]{1,0:T(8,128)(2,1)}, bf16[64,128,512]{2,1,0:T(8,128)(2,1)}, bf16[64,512,128]{2,1,0:T(8,128)(2,1)}, bf16[16,512]{1,0:T(8,128)(2,1)}, bf16[512,16]{1,0:T(8,128)(2,1)}) custom-call(bf16[2048,512]{1,0:T(8,128)(2,1)} %refs_1_.1, f32[1,512]{1,0:T(1,128)} %bitcast.4, bf16[512,512]{1,0:T(8,128)(2,1)} %wq.1, bf16[512,512]{1,0:T(8,128)(2,1)} %wk.1, ...), custom_call_target="tpu_custom_call" | custom-call | tf_op jit(solution)/shard_map/exchange/pallas_call | solution.py:487
  68.5 36.9 %attention.1 = bf16[2048,512]{1,0:T(8,128)(2,1)} custom-call(s32[6,16]{1,0:T(8,128)} %bitcast.3, s32[16]{0:T(128)} %counts.3, bf16[2048,512]{1,0:T(8,128)(2,1)} %get-tuple-element.10.refs_0_, bf16[2048,512]{1,0:T(8,128)(2,1)} %refs_1_.1, bf16[64,128,512]{2,1,0:T(8,128)(2,1)} %get-tuple-element.11.refs_2_.refs_3_.refs_4_.refs_5_.refs_6_.refs_7_, ...), custom_call_target="tpu_custom_call" | custom-call | tf_op jit(solution)/shard_map/attention/pallas_call | solution.py:543
